TPU v7x, 32 devices: a whole 2x2x4 slice. The times are simulated.
32 devices in a mesh: dp: 4 (over x, core), blk: 8 (over z, y).
Axes of the slice: x: 2, y: 2, z: 4, core: 2. Of those that a mesh axis runs over, the one named last changes fastest.
Arguments:
- frames: bfloat16 [4, 1024, 768], P('dp', 'blk'), may hold values from -6 to 6
- segment: int32 [4, 1024], P('dp', 'blk'), may hold values from -1 to 16, as said below
- conv_weight: bfloat16 [768, 48, 128], replicated, may hold values from -0.078125 to 0.078125
- conv_bias: bfloat16 [768], replicated, may hold values from -1.5 to 1.5
- qkv_weight: bfloat16 [768, 2304], replicated, may hold values from -0.21875 to 0.21875
- qv_bias: bfloat16 [1536], replicated, may hold values from -1.5 to 1.5
- out_weight: bfloat16 [768, 768], replicated, may hold values from -0.875 to 0.875
- out_bias: bfloat16 [768], replicated, may hold values from -1.5 to 1.5
- norm1_gain: bfloat16 [768], replicated, may hold values from 0.25 to 1.75
- norm1_bias: bfloat16 [768], replicated, may hold values from -1.5 to 1.5
- ffn_in: bfloat16 [768, 3072], replicated, may hold values from -0.21875 to 0.21875
- ffn_in_bias: bfloat16 [3072], replicated, may hold values from -1.5 to 1.5
- ffn_out: bfloat16 [3072, 768], replicated, may hold values from -0.109375 to 0.109375
- ffn_out_bias: bfloat16 [768], replicated, may hold values from -1.5 to 1.5
- norm2_gain: bfloat16 [768], replicated, may hold values from 0.25 to 1.75
- norm2_bias: bfloat16 [768], replicated, may hold values from -1.5 to 1.5
- cotangent: bfloat16 [4, 1024, 768], P('dp', 'blk'), may hold values from -6 to 6
Outputs:
- layer_out: bfloat16 [4, 1024, 768], P('dp', 'blk')
- frames_grad: bfloat16 [4, 1024, 768], P('dp', 'blk')
- conv_weight_grad: float32 [768, 48, 128], P('blk')
- conv_bias_grad: float32 [768], P('blk')
- qkv_weight_grad: float32 [768, 2304], P('blk')
- qv_bias_grad: float32 [1536], P('blk')
- out_weight_grad: float32 [768, 768], P('blk')
- out_bias_grad: float32 [768], P('blk')
- norm1_gain_grad: float32 [768], P('blk')
- norm1_bias_grad: float32 [768], P('blk')
- ffn_in_grad: float32 [768, 3072], P('blk')
- ffn_in_bias_grad: float32 [3072], P('blk')
- ffn_out_grad: float32 [3072, 768], P('blk')
- ffn_out_bias_grad: float32 [768], P('blk')
- norm2_gain_grad: float32 [768], P('blk')
- norm2_bias_grad: float32 [768], P('blk')
Inputs may be any that keep to these rules, and one draw needn't show every extreme that they name: `segment`: in each row the frames of a clip are consecutive and clips are numbered 0, 1, 2, ... in order; padding frames, if any, close the row. At least one row holds a clip that starts in the row's first 128 frames and ends in its last 128.
All inputs are finite; a program needn't handle non-finite values.
Results may differ from a plain program's by a relative error of at most 0.02.
Values may be sent and summed in bfloat16 or wider, within the bound.
A program may use at most 320 MiB of HBM per device.

v0:
```python
import math

import jax
import jax.numpy as jnp
from jax import lax
from jax.sharding import PartitionSpec as P

HEADS = 12
GROUPS = 16


EPS = 1e-05
ROOT_HALF = 0.7071067811865476
DENSITY_CONST = 0.3989422804014327


def with_halo(x, sides, width):
    for axis, dim in sides:
        size, length = (lax.axis_size(axis), x.shape[dim])
        up = [(i, (i + 1) % size) for i in range(size - 1)]
        down = [(j, i) for i, j in up]
        last = lax.slice_in_dim(x, length - width, length, axis=dim)
        initial = lax.slice_in_dim(x, 0, width, axis=dim)
        before = lax.ppermute(last, axis, up)
        after = lax.ppermute(initial, axis, down)
        x = jnp.concatenate([before, x, after], axis=dim)
    return x


def from_behind(value, axis, steps):
    count = lax.axis_size(axis)
    pairs = [(source, (source + steps) % count) for source in range(count)]
    return lax.ppermute(value, axis, pairs)


def gelu_value(signal):
    return 0.5 * signal * (1.0 + lax.erf(signal * ROOT_HALF))


def gelu_slope(signal):
    return (
        0.5 * (1.0 + lax.erf(signal * ROOT_HALF))
        + signal * jnp.exp(-0.5 * signal * signal) * DENSITY_CONST
    )


def norm_forward(signal, gain_vec, shift_vec):
    average = jnp.mean(signal, axis=-1, keepdims=True)
    centred = signal - average
    inv_std = lax.rsqrt(jnp.mean(centred * centred, axis=-1, keepdims=True) + EPS)
    normed = centred * inv_std
    return (normed * gain_vec + shift_vec, normed, inv_std)


def norm_backward(grad_in, normed, inv_std, gain_vec):
    scaled = grad_in * gain_vec
    result = inv_std * (
        scaled
        - jnp.mean(scaled, axis=-1, keepdims=True)
        - normed * jnp.mean(scaled * normed, axis=-1, keepdims=True)
    )
    return (result, jnp.sum(grad_in * normed, axis=0), jnp.sum(grad_in, axis=0))


def block_grads(
    query_h, dout_h, query_seg, log_tot, row_delta, key_h, value_h, key_seg, score_scale
):
    scores = (
        jnp.einsum("rqhc,rkhc->rhqk", query_h, key_h, preferred_element_type=jnp.float32)
        * score_scale
    )
    same_seg = (query_seg[:, :, None] == key_seg[:, None, :])[:, None]
    weights_f = jnp.where(same_seg, jnp.exp(scores - log_tot[..., None]), 0.0)
    grad_prob = jnp.einsum("rqhc,rkhc->rhqk", dout_h, value_h, preferred_element_type=jnp.float32)
    grad_score = (weights_f * (grad_prob - row_delta[..., None])).astype(jnp.bfloat16)
    query_part = score_scale * jnp.einsum(
        "rhqk,rkhc->rqhc", grad_score, key_h, preferred_element_type=jnp.float32
    )
    key_part = score_scale * jnp.einsum(
        "rhqk,rqhc->rkhc", grad_score, query_h, preferred_element_type=jnp.float32
    )
    value_part = jnp.einsum(
        "rhqk,rqhc->rkhc",
        weights_f.astype(jnp.bfloat16),
        dout_h,
        preferred_element_type=jnp.float32,
    )
    return (query_part, key_part, value_part)


def shards(
    frames,
    segment,
    conv_weight,
    conv_bias,
    qkv_weight,
    qv_bias,
    out_weight,
    out_bias,
    norm1_gain,
    norm1_bias,
    ffn_in,
    ffn_in_bias,
    ffn_out,
    ffn_out_bias,
    norm2_gain,
    norm2_bias,
    cotangent,
):
    row_count, block_len, model_width = frames.shape
    token_count = row_count * block_len
    group_width = conv_weight.shape[1]
    kernel = conv_weight.shape[2]
    half_kernel = kernel // 2
    head_dim = model_width // HEADS
    score_scale = head_dim ** (-0.5)
    cycle_len = lax.axis_size("blk")
    is_valid = segment >= 0
    masked = jnp.where(is_valid[..., None], frames, jnp.zeros_like(frames))
    padded = with_halo(masked, (("blk", 1),), half_kernel)
    conv_out = lax.conv_general_dilated(
        padded,
        conv_weight,
        (1,),
        "VALID",
        dimension_numbers=("NWC", "OIW", "NWC"),
        feature_group_count=GROUPS,
        preferred_element_type=jnp.float32,
    )
    pre_conv = conv_out[:, :block_len].reshape(token_count, model_width) + conv_bias.astype(
        jnp.float32
    )
    mixed_in = frames.reshape(token_count, model_width).astype(jnp.float32) + gelu_value(pre_conv)
    mixed_low = mixed_in.astype(jnp.bfloat16)
    pair_bias = qv_bias.astype(jnp.float32)
    zero_bias = jnp.zeros((model_width,), jnp.float32)
    full_bias = jnp.concatenate([pair_bias[:model_width], zero_bias, pair_bias[model_width:]])
    project = (
        jnp.dot(mixed_low, qkv_weight, preferred_element_type=jnp.float32) + full_bias
    ).astype(jnp.bfloat16)
    project = project.reshape(row_count, block_len, 3 * model_width)
    query_heads = project[..., :model_width].reshape(row_count, block_len, HEADS, head_dim)
    keys_local = project[..., model_width : 2 * model_width]
    values_local = project[..., 2 * model_width :]
    key_heads = keys_local.reshape(row_count, block_len, HEADS, head_dim)
    value_heads = values_local.reshape(row_count, block_len, HEADS, head_dim)
    query_seg = segment.astype(jnp.bfloat16)
    start_carry = (
        jnp.full((row_count, HEADS, block_len), -1e30, jnp.float32),
        jnp.zeros((row_count, HEADS, block_len), jnp.float32),
        jnp.zeros((row_count, HEADS, block_len, head_dim), jnp.float32),
    )
    key_piece = lax.all_gather(keys_local, "blk", axis=1, tiled=True)
    value_piece = lax.all_gather(values_local, "blk", axis=1, tiled=True)
    seg_piece = lax.all_gather(query_seg, "blk", axis=1, tiled=True)
    piece_len = key_piece.shape[1]
    block_size = math.gcd(piece_len, 512)

    def one_block(block_index, inner_carry):
        running_max, denominator, numerator = inner_carry
        offset = block_index * block_size
        key_block = lax.dynamic_slice_in_dim(key_piece, offset, block_size, 1).reshape(
            row_count, block_size, HEADS, head_dim
        )
        value_block = lax.dynamic_slice_in_dim(value_piece, offset, block_size, 1).reshape(
            row_count, block_size, HEADS, head_dim
        )
        seg_block = lax.dynamic_slice_in_dim(seg_piece, offset, block_size, 1)
        scores = (
            jnp.einsum(
                "rqhc,rkhc->rhqk", query_heads, key_block, preferred_element_type=jnp.float32
            )
            * score_scale
        )
        same_seg = (query_seg[:, :, None] == seg_block[:, None, :])[:, None]
        masked_scores = jnp.where(same_seg, scores, -1e30)
        new_max = jnp.maximum(running_max, jnp.max(masked_scores, axis=-1))
        weights_f = jnp.where(same_seg, jnp.exp(masked_scores - new_max[..., None]), 0.0)
        rescale = jnp.exp(running_max - new_max)
        denominator = denominator * rescale + jnp.sum(weights_f, axis=-1)
        numerator = numerator * rescale[..., None] + jnp.einsum(
            "rhqk,rkhc->rhqc",
            weights_f.astype(jnp.bfloat16),
            value_block,
            preferred_element_type=jnp.float32,
        )
        return (new_max, denominator, numerator)

    running_max, denominator, numerator = lax.fori_loop(
        0, piece_len // block_size, one_block, start_carry
    )
    log_total = running_max + jnp.log(denominator)
    attended_heads = (numerator / denominator[..., None]).transpose(0, 2, 1, 3)
    attended = attended_heads.reshape(token_count, model_width)
    attn_low = attended.astype(jnp.bfloat16)
    branch = jnp.dot(attn_low, out_weight, preferred_element_type=jnp.float32) + out_bias.astype(
        jnp.float32
    )
    gain_one = norm1_gain.astype(jnp.float32)
    hidden_norm, normed_one, inv_one = norm_forward(
        mixed_in + branch, gain_one, norm1_bias.astype(jnp.float32)
    )
    hidden_low = hidden_norm.astype(jnp.bfloat16)
    ffn_pre = jnp.dot(hidden_low, ffn_in, preferred_element_type=jnp.float32) + ffn_in_bias.astype(
        jnp.float32
    )
    ffn_act = gelu_value(ffn_pre).astype(jnp.bfloat16)
    ffn_branch = jnp.dot(
        ffn_act, ffn_out, preferred_element_type=jnp.float32
    ) + ffn_out_bias.astype(jnp.float32)
    gain_two = norm2_gain.astype(jnp.float32)
    layer_out, normed_two, inv_two = norm_forward(
        hidden_norm + ffn_branch, gain_two, norm2_bias.astype(jnp.float32)
    )
    grad_top = cotangent.reshape(token_count, model_width).astype(jnp.float32)
    grad_second, norm2_gain_grad, norm2_bias_grad = norm_backward(
        grad_top, normed_two, inv_two, gain_two
    )
    grad_branch_two = grad_second.astype(jnp.bfloat16)
    ffn_out_grad = jnp.einsum(
        "nf,nd->fd", ffn_act, grad_branch_two, preferred_element_type=jnp.float32
    )
    ffn_out_bias_grad = jnp.sum(grad_branch_two.astype(jnp.float32), axis=0)
    grad_act = jnp.einsum("nd,fd->nf", grad_branch_two, ffn_out, preferred_element_type=jnp.float32)
    grad_pre = (grad_act * gelu_slope(ffn_pre)).astype(jnp.bfloat16)
    ffn_in_grad = jnp.einsum("nd,nf->df", hidden_low, grad_pre, preferred_element_type=jnp.float32)
    ffn_in_bias_grad = jnp.sum(grad_pre.astype(jnp.float32), axis=0)
    grad_hidden = grad_second + jnp.einsum(
        "nf,df->nd", grad_pre, ffn_in, preferred_element_type=jnp.float32
    )
    grad_first, norm1_gain_grad, norm1_bias_grad = norm_backward(
        grad_hidden, normed_one, inv_one, gain_one
    )
    grad_branch = grad_first.astype(jnp.bfloat16)
    out_weight_grad = jnp.einsum(
        "ne,nd->ed", attn_low, grad_branch, preferred_element_type=jnp.float32
    )
    out_bias_grad = jnp.sum(grad_branch.astype(jnp.float32), axis=0)
    grad_att = jnp.einsum("nd,ed->ne", grad_branch, out_weight, preferred_element_type=jnp.float32)
    grad_heads = grad_att.astype(jnp.bfloat16).reshape(row_count, block_len, HEADS, head_dim)
    row_delta = jnp.einsum("rqhc,rqhc->rhq", grad_heads.astype(jnp.float32), attended_heads)
    zero_heads = jnp.zeros((row_count, block_len, HEADS, head_dim), jnp.float32)

    def key_step(carried):
        key_block, value_block, seg_block, key_grad, value_grad, query_grad = carried
        query_part, key_part, value_part = block_grads(
            query_heads,
            grad_heads,
            query_seg,
            log_total,
            row_delta,
            key_block,
            value_block,
            seg_block,
            score_scale,
        )
        query_grad = query_grad + query_part
        key_grad = key_grad + key_part
        value_grad = value_grad + value_part
        key_block, value_block, seg_block = from_behind(
            (key_block, value_block, seg_block), "blk", 1
        )
        key_grad, value_grad = (
            from_behind(key_grad.astype(jnp.bfloat16), "blk", 1).astype(key_grad.dtype),
            from_behind(value_grad.astype(jnp.bfloat16), "blk", 1).astype(value_grad.dtype),
        )
        return (key_block, value_block, seg_block, key_grad, value_grad, query_grad)

    def four_steps(turn_index, carried):
        for repeat in range(4):
            carried = key_step(carried)
        return carried

    final_state = lax.fori_loop(
        0,
        cycle_len // 4,
        four_steps,
        (key_heads, value_heads, query_seg, zero_heads, zero_heads, zero_heads),
    )
    key_grad, value_grad, query_grad = (final_state[3], final_state[4], final_state[5])
    grad_project = jnp.concatenate(
        [
            query_grad.reshape(token_count, model_width),
            key_grad.reshape(token_count, model_width),
            value_grad.reshape(token_count, model_width),
        ],
        axis=1,
    ).astype(jnp.bfloat16)
    qkv_weight_grad = jnp.einsum(
        "nd,ne->de", mixed_low, grad_project, preferred_element_type=jnp.float32
    )
    bias_sums = jnp.sum(grad_project.astype(jnp.float32), axis=0)
    qv_bias_grad = jnp.concatenate([bias_sums[:model_width], bias_sums[2 * model_width :]])
    grad_mixed = grad_first + jnp.einsum(
        "ne,de->nd", grad_project, qkv_weight, preferred_element_type=jnp.float32
    )
    grad_conv = (grad_mixed * gelu_slope(pre_conv)).astype(jnp.bfloat16)
    conv_bias_grad = jnp.sum(grad_conv.astype(jnp.float32), axis=0)
    grad_conv_rows = grad_conv.reshape(row_count, block_len, model_width)
    grad_padded = with_halo(grad_conv_rows, (("blk", 1),), half_kernel)
    flipped = conv_weight.reshape(GROUPS, group_width, group_width, kernel).transpose(0, 2, 1, 3)
    flipped = flipped.reshape(model_width, group_width, kernel)[:, :, ::-1]
    back_conv = lax.conv_general_dilated(
        grad_padded,
        flipped,
        (1,),
        "VALID",
        dimension_numbers=("NWC", "OIW", "NWC"),
        feature_group_count=GROUPS,
        preferred_element_type=jnp.float32,
    )[:, 1:]
    frames_grad = (
        grad_mixed.reshape(row_count, block_len, model_width)
        + jnp.where(is_valid[..., None], back_conv, 0.0)
    ).astype(jnp.bfloat16)
    conv_weight_grad = lax.conv_general_dilated(
        padded,
        grad_conv_rows,
        (1,),
        "VALID",
        dimension_numbers=("CWN", "IWO", "CNW"),
        batch_group_count=GROUPS,
        preferred_element_type=jnp.float32,
    )[:, :, :kernel]
    (
        conv_weight_part,
        conv_bias_part,
        qkv_weight_part,
        qv_bias_part,
        out_weight_part,
        out_bias_part,
        gain_one_part,
        shift_one_part,
        ffn_in_part,
        ffn_in_bias_part,
        ffn_out_part,
        ffn_out_bias_part,
        gain_two_part,
        shift_two_part,
    ) = (
        lax.psum_scatter(conv_weight_grad, "blk", scatter_dimension=0, tiled=True),
        lax.psum_scatter(conv_bias_grad, "blk", scatter_dimension=0, tiled=True),
        lax.psum_scatter(qkv_weight_grad, "blk", scatter_dimension=0, tiled=True),
        lax.psum_scatter(qv_bias_grad, "blk", scatter_dimension=0, tiled=True),
        lax.psum_scatter(out_weight_grad, "blk", scatter_dimension=0, tiled=True),
        lax.psum_scatter(out_bias_grad, "blk", scatter_dimension=0, tiled=True),
        lax.psum_scatter(norm1_gain_grad, "blk", scatter_dimension=0, tiled=True),
        lax.psum_scatter(norm1_bias_grad, "blk", scatter_dimension=0, tiled=True),
        lax.psum_scatter(ffn_in_grad, "blk", scatter_dimension=0, tiled=True),
        lax.psum_scatter(ffn_in_bias_grad, "blk", scatter_dimension=0, tiled=True),
        lax.psum_scatter(ffn_out_grad, "blk", scatter_dimension=0, tiled=True),
        lax.psum_scatter(ffn_out_bias_grad, "blk", scatter_dimension=0, tiled=True),
        lax.psum_scatter(norm2_gain_grad, "blk", scatter_dimension=0, tiled=True),
        lax.psum_scatter(norm2_bias_grad, "blk", scatter_dimension=0, tiled=True),
    )
    totals = (
        lax.psum(conv_weight_part.astype(jnp.bfloat16), "dp").astype(jnp.float32),
        lax.psum(conv_bias_part.astype(jnp.bfloat16), "dp").astype(jnp.float32),
        lax.psum(qkv_weight_part.astype(jnp.bfloat16), "dp").astype(jnp.float32),
        lax.psum(qv_bias_part.astype(jnp.bfloat16), "dp").astype(jnp.float32),
        lax.psum(out_weight_part.astype(jnp.bfloat16), "dp").astype(jnp.float32),
        lax.psum(out_bias_part.astype(jnp.bfloat16), "dp").astype(jnp.float32),
        lax.psum(gain_one_part.astype(jnp.bfloat16), "dp").astype(jnp.float32),
        lax.psum(shift_one_part.astype(jnp.bfloat16), "dp").astype(jnp.float32),
        lax.psum(ffn_in_part.astype(jnp.bfloat16), "dp").astype(jnp.float32),
        lax.psum(ffn_in_bias_part.astype(jnp.bfloat16), "dp").astype(jnp.float32),
        lax.psum(ffn_out_part.astype(jnp.bfloat16), "dp").astype(jnp.float32),
        lax.psum(ffn_out_bias_part.astype(jnp.bfloat16), "dp").astype(jnp.float32),
        lax.psum(gain_two_part.astype(jnp.bfloat16), "dp").astype(jnp.float32),
        lax.psum(shift_two_part.astype(jnp.bfloat16), "dp").astype(jnp.float32),
    )
    return (
        layer_out.reshape(row_count, block_len, model_width).astype(jnp.bfloat16),
        frames_grad,
        totals[0],
        totals[1],
        totals[2],
        totals[3],
        totals[4],
        totals[5],
        totals[6],
        totals[7],
        totals[8],
        totals[9],
        totals[10],
        totals[11],
        totals[12],
        totals[13],
    )


def solution(mesh):
    return jax.shard_map(
        shards,
        mesh=mesh,
        in_specs=(
            P("dp", "blk", None),
            P("dp", "blk"),
            P(),
            P(),
            P(),
            P(),
            P(),
            P(),
            P(),
            P(),
            P(),
            P(),
            P(),
            P(),
            P(),
            P(),
            P("dp", "blk", None),
        ),
        out_specs=(
            P("dp", "blk", None),
            P("dp", "blk", None),
            P("blk", None, None),
            P("blk"),
            P("blk", None),
            P("blk"),
            P("blk", None),
            P("blk"),
            P("blk"),
            P("blk"),
            P("blk", None),
            P("blk"),
            P("blk", None),
            P("blk"),
            P("blk"),
            P("blk"),
        ),
        check_vma=False,
    )
```

profile of v0, /device:TPU:0, one launch (start us, length us, event | category | flops | bytes accessed | tf_op | source)
XLA Modules:
  0.0 1527.3 jit_solution(10102650907398600749)
XLA Ops:
  19.5 33.9 %copy.111 = bf16[16,48,48,128]{2,1,0,3:T(8,128)(2,1)} copy(bf16[16,48,48,128]{3,2,1,0:T(8,128)(2,1)} %bitcast.478) | data formatting | bytes 18874368 | tf_op jit(solution)/shard_map/shard_map
  63.1 168.2 %convolution_reduce_fusion = f32[129,16,48]{2,1,0:T(8,128)} fusion(bf16[1,256,16,48]{3,0,2,1:T(2,128)(2,1)} %copy.110, bf16[16,48,48,128]{2,1,0,3:T(8,128)(2,1)} %copy.111), kind=kOutput, calls=%fused_computation.150 | convolution fusion | flops 1217396736 | bytes 10226688 | tf_op jit(solution)/shard_map/conv_general_dilated | solution.py:121
  248.4 22.6 %all_gather.9 = bf16[1,1024]{1,0:T(2,128)(2,1)} all-gather(bf16[1,128]{1,0:T(2,128)(2,1)} %convert_element_type.276), channel_id=1, replica_groups=mesh['dp'=4,'blk'=8] {'blk'}, dimensions={1}, use_global_device_ids=true | all-gather | bytes 2304 | tf_op jit(solution)/shard_map/all_gather | solution.py:155
  276.3 6.8 all-gather.5.cloned.1.call-done
  283.1 45.8 %all-gather.3.cloned.1.call-done = bf16[1,1024,768]{2,1,0:T(8,128)(2,1)} async-done(((bf16[1,128,768]{2,1,0:T(8,128)(2,1)}), bf16[1,1024,768]{2,1,0:T(8,128)(2,1)}) %all-gather.3.cloned.1.call-update) | async-done | bytes 1572880 | tf_op jit(solution)/shard_map/all_gather | solution.py:153
  328.9 26.9 %while.39 = (s32[]{:T(128)}, f32[1,12,128]{2,1,0:T(8,128)S(1)}, f32[1,12,128]{2,1,0:T(8,128)S(1)}, f32[1,12,128,64]{2,3,1,0:T(8,128)}, bf16[1,128]{1,0:T(2,128)(...) while((s32[]{:T(128)}, f32[1,12,128]{2,1,0:T(8,128)S(1)}, ...), condition=%wide.region_3.4_spmd.clone, body=%wide.region_0.3_spmd.clone.sunk | while | flops 211919872 | bytes 25202228 | solution.py:189
  381.1 189.3 %while.40 = (s32[]{:T(128)}, bf16[1,128,12,64]{1,3,2,0:T(8,128)(2,1)}, bf16[1,128,12,64]{1,3,2,0:T(8,128)(2,1)}, bf16[1,128]{1,0:T(2,128)(2,1)}, f32[1,128,12,64...) while((s32[]{:T(128)}, ...), condition=%wide.region_13.14_spmd.clone, body=%wide.region_12.13_spmd.clone.sunk | while | flops 512720896 | bytes 50569668 | solution.py:274
  395.0 7.7 collective-permute-done.10
  460.9 11.2 collective-permute-done.15
  489.3 6.5 collective-permute-done.10
  506.7 8.6 collective-permute-done.12
  556.2 10.6 collective-permute-done.15
  579.5 6.7 fusion.141
  600.8 205.0 %fusion.156 = f32[16,48,48,129]{1,2,0,3:T(8,128)} fusion(bf16[1,256,16,48]{3,0,2,1:T(2,128)(2,1)S(1)} %copy-done.20, bf16[1,128,16,48]{3,0,2,1:T(2,128)(2,1)S(1)} %copy.121), kind=kOutput, calls=%fused_computation.246 | convolution fusion | flops 1217396736 | bytes 19611648 | tf_op jit(solution)/shard_map/conv_general_dilated | solution.py:316
  805.8 42.3 %copy.127 = f32[16,48,48,129]{1,0,2,3:T(8,128)} copy(f32[16,48,48,129]{1,2,0,3:T(8,128)} %fusion.156) | data formatting | bytes 38043648 | tf_op jit(solution)/shard_map/conv_general_dilated | solution.py:316
  848.1 40.7 %conv_general_dilated.20 = f32[768,48,129]{0,1,2:T(8,128)} reshape(f32[16,48,48,129]{1,0,2,3:T(8,128)} %copy.127) | data formatting | bytes 38043648 | tf_op jit(solution)/shard_map/conv_general_dilated | solution.py:316
  888.8 14.6 slice.67
  903.4 19.1 %copy.128 = f32[768,48,128]{2,1,0:T(8,128)} copy(f32[768,48,128]{0,1,2:T(8,128)} %slice.67) | data formatting | bytes 37748736 | tf_op jit(solution)/shard_map/slice | solution.py:316
  925.7 9.8 copy.123
  935.5 23.9 %rev.5 = bf16[768,48,128]{2,1,0:T(8,128)(2,1)} reverse(bf16[768,48,128]{2,1,0:T(8,128)(2,1)} %bitcast.477), dimensions={2} | reverse | bytes 18874368 | tf_op jit(solution)/shard_map/rev | solution.py:302
  959.5 34.0 %copy.124 = bf16[16,48,48,128]{2,1,0,3:T(8,128)(2,1)} copy(bf16[16,48,48,128]{3,2,1,0:T(8,128)(2,1)} %bitcast.480) | data formatting | bytes 18874368 | tf_op jit(solution)/shard_map/rev | solution.py:302
  996.6 38.8 %all-reduce.9 = (bf16[768]{0:T(1024)(128)(2,1)S(1)}, bf16[1536]{0:T(1024)(128)(2,1)S(1)}, bf16[768]{0:T(1024)(128)(2,1)S(1)}, bf16[768]{0:T(1024)(128)(2,1)S(1)}...) all-reduce(f32[768]{0:T(1024)S(1)} %copy-done.60, ...), channel_id=3, replica_groups=mesh['dp'=4,'blk'=8] {'blk'}, use_global_device_ids=true, to_apply=%region_17.18.clone | all-reduce | flops 9984 | bytes 59904
  1056.5 300.5 %reduce-scatter.6.cloned.1.call-done = f32[96,48,128]{2,1,0:T(8,128)} async-done(((f32[768,48,128]{2,1,0:T(8,128)}), f32[96,48,128]{2,1,0:T(8,128)}) %reduce-scatter.6.cloned.1.call-update) | async-done | bytes 2359312 | tf_op jit(solution)/shard_map/reduce_scatter | solution.py:341
  1359.8 151.6 %fusion.110 = f32[129,16,48]{2,1,0:T(8,128)S(1)} fusion(bf16[16,48,48,128]{2,1,0,3:T(8,128)(2,1)} %copy.124, bf16[1,64,16,48]{3,0,2,1:T(2,128)(2,1)S(1)} %concatenate.35, bf16[1,128,16,48]{3,0,2,1:T(2,128)(2,1)S(1)} %copy.121, bf16[1,64,16,48]{3,0,2,1:T(2,128)(2,1)} %concatenate.34), kind=kOutput, calls=%fused_computation.159 | convolution fusion | flops 1218576384 | bytes 10226688 | tf_op jit(solution)/shard_map/conv_general_dilated | solution.py:303
  (443 shorter events, 300.1 us)
Async XLA Ops:
  7.2 275.9 %all-gather.5.cloned.1.call-start = ((), (), s32[]{:S(2)}) async-start(), calls=%async_computation.6 | async-start | bytes 1769472 | tf_op jit(solution)/shard_map/all_gather | solution.py:154
  10.6 43.3 %collective-permute-start.20 = (bf16[1,64,768]{2,1,0:T(8,128)(2,1)}, bf16[1,64,768]{2,1,0:T(8,128)(2,1)}, u32[]{:S(2)}, u32[]{:S(2)}) collective-permute-start(bf16[1,64,768]{2,1,0:T(8,128)(2,1)} %get-tuple-element.494), channel_id=1, source_target_pairs={{0,1},{1,2},{2,3},{3,4},{4,5},{5,6},{6,7},{8,9},{9,10},{10,11},{11... | collective-permute-start | bytes 294920 | tf_op jit(solution)/shard_map/ppermute | solution.py:24
  16.1 37.8 %collective-permute-start.21 = (bf16[1,64,768]{2,1,0:T(8,128)(2,1)}, bf16[1,64,768]{2,1,0:T(8,128)(2,1)}, u32[]{:S(2)}, u32[]{:S(2)}) collective-permute-start(bf16[1,64,768]{2,1,0:T(8,128)(2,1)} %get-tuple-element.495), channel_id=1, source_target_pairs={{1,0},{2,1},{3,2},{4,3},{5,4},{6,5},{7,6},{9,8},{10,9},{11,10},{12... | collective-permute-start | bytes 294920 | tf_op jit(solution)/shard_map/ppermute | solution.py:25
  236.3 92.5 %all-gather.3.cloned.1.call-start = ((), (), s32[]{:S(2)}) async-start(), calls=%async_computation.5 | async-start | bytes 1769472 | tf_op jit(solution)/shard_map/all_gather | solution.py:153
  237.1 811.2 %reduce-scatter.10.cloned.1.call-start = ((), (), s32[]{:S(2)}) async-start(), calls=%async_computation.9 | async-start | bytes 2654208 | tf_op jit(solution)/shard_map/reduce_scatter | solution.py:345
  381.1 668.8 %reduce-scatter.8.cloned.1.call-start = ((), (), s32[]{:S(2)}) async-start(), calls=%async_computation.8 | async-start | bytes 7962624 | tf_op jit(solution)/shard_map/reduce_scatter | solution.py:343
  382.2 30.0 %collective-permute-start.4 = (bf16[1,128,12,64]{1,3,2,0:T(8,128)(2,1)}, bf16[1,128,12,64]{1,3,2,0:T(8,128)(2,1)}, u32[]{:S(2)}, u32[]{:S(2)}) collective-permute-start(bf16[1,128,12,64]{1,3,2,0:T(8,128)(2,1)} %get-tuple-element.713), channel_id=1, source_target_pairs={{0,1},{1,2},{2,3},{3,4},{4,5},{5,6},{6,7},{7,0},{8,9},{9,10},{10,1... | collective-permute-start | bytes 589832 | tf_op jit(solution)/shard_map/while/body/eval_jaxpr/ppermute | solution.py:33
  407.2 68.1 %collective-permute-start.11 = (bf16[1,128]{1,0:T(2,128)(2,1)}, bf16[1,128]{1,0:T(2,128)(2,1)S(1)}, u32[]{:S(2)}, u32[]{:S(2)}) collective-permute-start(bf16[1,128]{1,0:T(2,128)(2,1)} %collective-permute-done.10), channel_id=1, source_target_pairs={{0,1},{1,2},{2,3},{3,4},{4,5},{5,6},{6,7},{7,0},{8,9},{9,10},{10,1... | collective-permute-start | bytes 776 | tf_op jit(solution)/shard_map/while/body/eval_jaxpr/ppermute | solution.py:33
  407.7 22.3 %collective-permute-start.1 = (bf16[1,128,12,64]{1,3,2,0:T(8,128)(2,1)}, bf16[1,128,12,64]{1,3,2,0:T(8,128)(2,1)S(1)}, u32[]{:S(2)}, u32[]{:S(2)}) collective-permute-start(bf16[1,128,12,64]{1,3,2,0:T(8,128)(2,1)} %collective-permute-done), channel_id=1, source_target_pairs={{0,1},{1,2},{2,3},{3,4},{4,5},{5,6},{6,7},{7,0},{8,9},{9,10},{10,1... | collective-permute-start | bytes 589832 | tf_op jit(solution)/shard_map/while/body/eval_jaxpr/ppermute | solution.py:33
  412.2 22.0 %collective-permute-start.5 = (bf16[1,128,12,64]{1,3,2,0:T(8,128)(2,1)}, bf16[1,128,12,64]{1,3,2,0:T(8,128)(2,1)S(1)}, u32[]{:S(2)}, u32[]{:S(2)}) collective-permute-start(bf16[1,128,12,64]{1,3,2,0:T(8,128)(2,1)} %collective-permute-done.4), channel_id=1, source_target_pairs={{0,1},{1,2},{2,3},{3,4},{4,5},{5,6},{6,7},{7,0},{8,9},{9,10},{10,1... | collective-permute-start | bytes 589832 | tf_op jit(solution)/shard_map/while/body/eval_jaxpr/ppermute | solution.py:33
  446.8 28.5 %collective-permute-start.3 = (bf16[1,128,12,64]{1,3,2,0:T(8,128)(2,1)S(1)}, bf16[1,128,12,64]{1,3,2,0:T(8,128)(2,1)S(1)}, u32[]{:S(2)}, u32[]{:S(2)}) collective-permute-start(bf16[1,128,12,64]{1,3,2,0:T(8,128)(2,1)S(1)} %collective-permute-done.2), channel_id=1, source_target_pairs={{0,1},{1,2},{2,3},{3,4},{4,5},{5,6},{6,7},{7,0},{8,9},{9,10},{10,1... | collective-permute-start | bytes 589832 | tf_op jit(solution)/shard_map/while/body/eval_jaxpr/ppermute | solution.py:33
  451.0 24.3 %collective-permute-start.7 = (bf16[1,128,12,64]{1,3,2,0:T(8,128)(2,1)S(1)}, bf16[1,128,12,64]{1,3,2,0:T(8,128)(2,1)S(1)}, u32[]{:S(2)}, u32[]{:S(2)}) collective-permute-start(bf16[1,128,12,64]{1,3,2,0:T(8,128)(2,1)S(1)} %collective-permute-done.6), channel_id=1, source_target_pairs={{0,1},{1,2},{2,3},{3,4},{4,5},{5,6},{6,7},{7,0},{8,9},{9,10},{10,1... | collective-permute-start | bytes 589832 | tf_op jit(solution)/shard_map/while/body/eval_jaxpr/ppermute | solution.py:33
  476.1 26.3 %collective-permute-start.4 = (bf16[1,128,12,64]{1,3,2,0:T(8,128)(2,1)}, bf16[1,128,12,64]{1,3,2,0:T(8,128)(2,1)}, u32[]{:S(2)}, u32[]{:S(2)}) collective-permute-start(bf16[1,128,12,64]{1,3,2,0:T(8,128)(2,1)} %get-tuple-element.713), channel_id=1, source_target_pairs={{0,1},{1,2},{2,3},{3,4},{4,5},{5,6},{6,7},{7,0},{8,9},{9,10},{10,1... | collective-permute-start | bytes 589832 | tf_op jit(solution)/shard_map/while/body/eval_jaxpr/ppermute | solution.py:33
  500.4 69.3 %collective-permute-start.11 = (bf16[1,128]{1,0:T(2,128)(2,1)}, bf16[1,128]{1,0:T(2,128)(2,1)S(1)}, u32[]{:S(2)}, u32[]{:S(2)}) collective-permute-start(bf16[1,128]{1,0:T(2,128)(2,1)} %collective-permute-done.10), channel_id=1, source_target_pairs={{0,1},{1,2},{2,3},{3,4},{4,5},{5,6},{6,7},{7,0},{8,9},{9,10},{10,1... | collective-permute-start | bytes 776 | tf_op jit(solution)/shard_map/while/body/eval_jaxpr/ppermute | solution.py:33
  500.9 24.3 %collective-permute-start.1 = (bf16[1,128,12,64]{1,3,2,0:T(8,128)(2,1)}, bf16[1,128,12,64]{1,3,2,0:T(8,128)(2,1)S(1)}, u32[]{:S(2)}, u32[]{:S(2)}) collective-permute-start(bf16[1,128,12,64]{1,3,2,0:T(8,128)(2,1)} %collective-permute-done), channel_id=1, source_target_pairs={{0,1},{1,2},{2,3},{3,4},{4,5},{5,6},{6,7},{7,0},{8,9},{9,10},{10,1... | collective-permute-start | bytes 589832 | tf_op jit(solution)/shard_map/while/body/eval_jaxpr/ppermute | solution.py:33
  502.3 27.1 %collective-permute-start.5 = (bf16[1,128,12,64]{1,3,2,0:T(8,128)(2,1)}, bf16[1,128,12,64]{1,3,2,0:T(8,128)(2,1)S(1)}, u32[]{:S(2)}, u32[]{:S(2)}) collective-permute-start(bf16[1,128,12,64]{1,3,2,0:T(8,128)(2,1)} %collective-permute-done.4), channel_id=1, source_target_pairs={{0,1},{1,2},{2,3},{3,4},{4,5},{5,6},{6,7},{7,0},{8,9},{9,10},{10,1... | collective-permute-start | bytes 589832 | tf_op jit(solution)/shard_map/while/body/eval_jaxpr/ppermute | solution.py:33
  542.1 27.6 %collective-permute-start.3 = (bf16[1,128,12,64]{1,3,2,0:T(8,128)(2,1)S(1)}, bf16[1,128,12,64]{1,3,2,0:T(8,128)(2,1)S(1)}, u32[]{:S(2)}, u32[]{:S(2)}) collective-permute-start(bf16[1,128,12,64]{1,3,2,0:T(8,128)(2,1)S(1)} %collective-permute-done.2), channel_id=1, source_target_pairs={{0,1},{1,2},{2,3},{3,4},{4,5},{5,6},{6,7},{7,0},{8,9},{9,10},{10,1... | collective-permute-start | bytes 589832 | tf_op jit(solution)/shard_map/while/body/eval_jaxpr/ppermute | solution.py:33
  546.3 23.4 %collective-permute-start.7 = (bf16[1,128,12,64]{1,3,2,0:T(8,128)(2,1)S(1)}, bf16[1,128,12,64]{1,3,2,0:T(8,128)(2,1)S(1)}, u32[]{:S(2)}, u32[]{:S(2)}) collective-permute-start(bf16[1,128,12,64]{1,3,2,0:T(8,128)(2,1)S(1)} %collective-permute-done.6), channel_id=1, source_target_pairs={{0,1},{1,2},{2,3},{3,4},{4,5},{5,6},{6,7},{7,0},{8,9},{9,10},{10,1... | collective-permute-start | bytes 589832 | tf_op jit(solution)/shard_map/while/body/eval_jaxpr/ppermute | solution.py:33
  579.5 472.7 %reduce-scatter.14.cloned.1.call-start = ((), (), s32[]{:S(2)}) async-start(), calls=%async_computation.11 | async-start | bytes 10616832 | tf_op jit(solution)/shard_map/reduce_scatter | solution.py:351
  586.3 468.0 %reduce-scatter.12.cloned.1.call-start = ((), (), s32[]{:S(2)}) async-start(), calls=%async_computation.10 | async-start | bytes 10616832 | tf_op jit(solution)/shard_map/reduce_scatter | solution.py:349
  599.2 757.8 %reduce-scatter.6.cloned.1.call-start = ((), (), s32[]{:S(2)}) async-start(), calls=%async_computation.7 | async-start | bytes 21233664 | tf_op jit(solution)/shard_map/reduce_scatter | solution.py:341
  922.5 590.3 %all-reduce.14.cloned.1.call-start = ((), (), s32[]{:S(2)}) async-start(), calls=%async_computation.12 | async-start | bytes 5898240 | tf_op jit(solution)/shard_map/psum | solution.py:357
  993.6 53.4 %collective-permute-start.22 = (bf16[1,64,768]{2,1,0:T(8,128)(2,1)S(1)}, bf16[1,64,768]{2,1,0:T(8,128)(2,1)S(1)}, u32[]{:S(2)}, u32[]{:S(2)}) collective-permute-start(bf16[1,64,768]{2,1,0:T(8,128)(2,1)S(1)} %get-tuple-element.492), channel_id=1, source_target_pairs={{0,1},{1,2},{2,3},{3,4},{4,5},{5,6},{6,7},{8,9},{9,10},{10,11},{11... | collective-permute-start | bytes 294920 | tf_op jit(solution)/shard_map/ppermute | solution.py:24
  994.9 51.6 %collective-permute-start.23 = (bf16[1,64,768]{2,1,0:T(8,128)(2,1)S(1)}, bf16[1,64,768]{2,1,0:T(8,128)(2,1)S(1)}, u32[]{:S(2)}, u32[]{:S(2)}) collective-permute-start(bf16[1,64,768]{2,1,0:T(8,128)(2,1)S(1)} %get-tuple-element.493), channel_id=1, source_target_pairs={{1,0},{2,1},{3,2},{4,3},{5,4},{6,5},{7,6},{9,8},{10,9},{11,10},{12... | collective-permute-start | bytes 294920 | tf_op jit(solution)/shard_map/ppermute | solution.py:25
  (110 other events, 1977.8 us)
Sparse Core Ops, SparseCore 0:
  236.5 46.5 all-gather.4
  285.8 42.9 all-gather.2
  381.2 131.4 reduce-scatter.9
  579.6 126.2 reduce-scatter.7
  709.8 162.5 reduce-scatter.13
  876.2 163.8 reduce-scatter.11
  1044.5 312.4 reduce-scatter.5
  1361.0 65.1 all-reduce.13
where the time goes:
time: 1530 us
  matrix products  597 us (39%)
  waiting for transfers between devices  497 us (32%)
  local copies, waits for them, and re-layouts  267 us (17%)
  blocking collectives  67.1 us (4%)
  other arithmetic  59.1 us (4%)
  starting transfers between devices  22 us (1%)
  between operations  17.1 us (1%)
    reduce_scatter x1, waiting for transfers between devices, shards(): lax.psum_scatter(conv_weight_grad, 'blk', scatter_dimension=0, tiled=True)  301 us
    conv_general_dilated x1, matrix products, shards(): lax.conv_general_dilated(padded, grad_conv_rows, (1,), 'VALID', dimension...  205 us
    conv_general_dilated x1, matrix products, shards(): lax.conv_general_dilated(padded, conv_weight, (1,), 'VALID', dimension_nu...  168 us
    conv_general_dilated x1, matrix products, shards(): lax.conv_general_dilated(grad_padded, flipped, (1,), 'VALID', dimension_n...  152 us
    ppermute x40, waiting for transfers between devices, from_behind(): return lax.ppermute(value, axis, pairs)  143 us
    conv_general_dilated x2, local copies, waits for them, and re-layouts, shards(): lax.conv_general_dilated(padded, grad_conv_rows, (1,), 'VALID', dimension...  83 us
    rev x2, local copies, waits for them, and re-layouts, shards(): flipped = flipped.reshape(model_width, group_width, kernel)[:, :, ::-1]  57.9 us
    all_gather x1, waiting for transfers between devices, shards(): key_piece = lax.all_gather(keys_local, 'blk', axis=1, tiled=True)  45.8 us
  transfers between devices with their start and end apart: 52, of which 33 were waited for; matrix products, arithmetic and copies ran while one was open for 44% of the time, Pallas kernels for 0%

commit v1 on v0

--- a/solution.py
+++ b/solution.py
@@ -1,8 +1,11 @@
+import functools
 import math
 
 import jax
 import jax.numpy as jnp
 from jax import lax
+from jax.experimental import pallas as pl
+from jax.experimental.pallas import tpu as pltpu
 from jax.sharding import PartitionSpec as P
 
 HEADS = 12
@@ -88,7 +91,7 @@
     return (query_part, key_part, value_part)
 
 
-def shards(
+def ring_shards(
     frames,
     segment,
     conv_weight,
@@ -389,9 +392,914 @@
     )
 
 
+MESH = pl.DeviceIdType.MESH
+LANES = 128
+TAP_STEP = 16
+VMEM = pl.BlockSpec(memory_space=pltpu.VMEM)
+
+
+def peer(me, step, count):
+    return lax.rem(me + step, count)
+
+
+def greet(me, count):
+    barrier = pltpu.get_barrier_semaphore()
+    for step in range(1, count):
+        pl.semaphore_signal(
+            barrier, inc=1, device_id={"blk": peer(me, step, count)}, device_id_type=MESH
+        )
+    pl.semaphore_wait(barrier, count - 1)
+
+
+def remote(src, dst, send_sem, recv_sem, target):
+    copy = pltpu.make_async_remote_copy(
+        src_ref=src,
+        dst_ref=dst,
+        send_sem=send_sem,
+        recv_sem=recv_sem,
+        device_id={"blk": target},
+        device_id_type=MESH,
+    )
+    copy.start()
+    return copy
+
+
+def lane_block(index):
+    return pl.ds(pl.multiple_of(index * LANES, LANES), LANES)
+
+
+def row_block(index, size):
+    return pl.ds(pl.multiple_of(index * size, size), size)
+
+
+def swap_blocks(tiles, width):
+    count = len(tiles)
+    lane = lax.broadcasted_iota(jnp.int32, tiles[0].shape, 1) // width
+    tiles = list(tiles)
+    step = count // 2
+    while step:
+        low = (lane & step) == 0
+        for u in range(count):
+            if u & step == 0:
+                one, two = tiles[u], tiles[u + step]
+                tiles[u] = jnp.where(low, one, pltpu.roll(two, step * width, 1))
+                tiles[u + step] = jnp.where(low, pltpu.roll(one, LANES - step * width, 1), two)
+        step //= 2
+    return tiles
+
+
+def spread_taps(source, offset, direction, stage_ref, out_ref):
+    rows, length = source.shape
+    blocks = out_ref.shape[1] // LANES
+    for tap in range(TAP_STEP):
+        shift = (length - offset - direction * tap) % length
+        moved = pltpu.roll(source, shift, 1)
+        for block in range(blocks):
+            stage_ref[block, pl.ds(tap, rows, stride=TAP_STEP), :] = moved[
+                :, block * LANES : (block + 1) * LANES
+            ]
+    for block in range(blocks):
+        out_ref[:, block * LANES : (block + 1) * LANES] = stage_ref[block].astype(jnp.bfloat16)
+
+
+def conv_forward_kernel(
+    count,
+    frames_ref,
+    seg_ref,
+    weight_ref,
+    pre_ref,
+    column_ref,
+    segs_ref,
+    turned_ref,
+    result_ref,
+    back_ref,
+    stage_ref,
+    taps_ref,
+    mix_ref,
+    send_one,
+    recv_one,
+    send_two,
+    recv_two,
+    send_seg,
+    recv_seg,
+):
+    me = lax.axis_index("blk")
+    groups, width = weight_ref.shape[0], weight_ref.shape[1]
+    channels = groups * width
+    steps = LANES // TAP_STEP
+    length = count * LANES
+    valid = (seg_ref[...] >= 0).astype(jnp.float32)
+    turned_ref[...] = (frames_ref[...].astype(jnp.float32).T * valid).astype(jnp.bfloat16)
+    greet(me, count)
+    copies = []
+    for step in range(1, count):
+        target = peer(me, step, count)
+        copies.append(
+            remote(
+                turned_ref.at[row_block(target, channels), :],
+                column_ref.at[:, lane_block(me + 1)],
+                send_one.at[step],
+                recv_one.at[step],
+                target,
+            )
+        )
+        copies.append(
+            remote(seg_ref, segs_ref.at[me], send_seg.at[step], recv_seg.at[step], target)
+        )
+    column_ref[:, lane_block(me + 1)] = turned_ref[row_block(me, channels), :]
+    column_ref[:, :LANES] = jnp.zeros((channels, LANES), jnp.bfloat16)
+    column_ref[:, length + LANES :] = jnp.zeros((channels, LANES), jnp.bfloat16)
+    segs_ref[me] = seg_ref[...]
+    for group in range(groups):
+        for block in range(width // steps):
+            tiles = [
+                weight_ref[group, block * steps + u].astype(jnp.float32) for u in range(steps)
+            ]
+            for a, tile in enumerate(swap_blocks(tiles, TAP_STEP)):
+                mix_ref[
+                    group, a * width : (a + 1) * width, block * LANES : (block + 1) * LANES
+                ] = tile.astype(jnp.bfloat16)
+    for copy in copies:
+        copy.wait()
+    for group in range(groups):
+        rows = slice(group * width, (group + 1) * width)
+        source = column_ref[rows, :].astype(jnp.float32)
+        spread_taps(source, LANES // 2, 1, stage_ref, taps_ref)
+        product = jnp.dot(mix_ref[group], taps_ref[...], preferred_element_type=jnp.float32)
+        total = product[:width, :length]
+        span = product.shape[1]
+        for a in range(1, steps):
+            part = pltpu.roll(
+                product[a * width : (a + 1) * width, :], span - a * TAP_STEP, 1
+            )
+            total = total + part[:, :length]
+        result_ref[rows, :] = total
+    copies = []
+    for step in range(1, count):
+        target = peer(me, step, count)
+        copies.append(
+            remote(
+                result_ref.at[:, lane_block(target)],
+                back_ref.at[row_block(me, channels), :],
+                send_two.at[step],
+                recv_two.at[step],
+                target,
+            )
+        )
+    back_ref[row_block(me, channels), :] = result_ref[:, lane_block(me)]
+    for copy in copies:
+        copy.wait()
+    pre_ref[...] = back_ref[...].T
+
+
+def conv_forward(frames, seg, weight, count):
+    tokens, features = frames.shape
+    groups, width, _, kernel = weight.shape
+    channels = groups * width
+    length = count * LANES
+    span = length + LANES
+    rows = width * TAP_STEP
+    steps = kernel // TAP_STEP
+    sems = [pltpu.SemaphoreType.DMA((count,)) for _ in range(6)]
+    return pl.pallas_call(
+        functools.partial(conv_forward_kernel, count),
+        out_shape=(
+            jax.ShapeDtypeStruct((tokens, features), jnp.float32),
+            jax.ShapeDtypeStruct((channels, span + LANES), jnp.bfloat16),
+            jax.ShapeDtypeStruct((count, 1, LANES), jnp.int32),
+        ),
+        in_specs=[VMEM] * 3,
+        out_specs=(VMEM,) * 3,
+        scratch_shapes=[
+            pltpu.VMEM((features, tokens), jnp.bfloat16),
+            pltpu.VMEM((channels, length), jnp.float32),
+            pltpu.VMEM((features, tokens), jnp.float32),
+            pltpu.VMEM((span // LANES, rows, LANES), jnp.float32),
+            pltpu.VMEM((rows, span), jnp.bfloat16),
+            pltpu.VMEM((groups, steps * width, rows), jnp.bfloat16),
+        ]
+        + sems,
+        compiler_params=pltpu.CompilerParams(
+            collective_id=0, has_side_effects=True, vmem_limit_bytes=48 * 2**20
+        ),
+        name="conv_forward",
+    )(frames, seg, weight)
+
+
+def conv_backward_kernel(
+    count,
+    grad_ref,
+    column_ref,
+    weight_ref,
+    back_ref,
+    dweight_ref,
+    turned_ref,
+    gcol_ref,
+    result_ref,
+    home_ref,
+    stage_ref,
+    taps_ref,
+    mix_ref,
+    shifted_ref,
+    send_one,
+    recv_one,
+    send_two,
+    recv_two,
+):
+    me = lax.axis_index("blk")
+    channels, width = weight_ref.shape[0], weight_ref.shape[1]
+    groups = channels // width
+    steps = LANES // TAP_STEP
+    length = count * LANES
+    turned_ref[...] = grad_ref[...].astype(jnp.float32).T.astype(jnp.bfloat16)
+    greet(me, count)
+    copies = []
+    for step in range(1, count):
+        target = peer(me, step, count)
+        copies.append(
+            remote(
+                turned_ref.at[row_block(target, channels), :],
+                gcol_ref.at[:, lane_block(me + 1)],
+                send_one.at[step],
+                recv_one.at[step],
+                target,
+            )
+        )
+    gcol_ref[:, lane_block(me + 1)] = turned_ref[row_block(me, channels), :]
+    gcol_ref[:, :LANES] = jnp.zeros((channels, LANES), jnp.bfloat16)
+    gcol_ref[:, length + LANES :] = jnp.zeros((channels, LANES), jnp.bfloat16)
+    for group in range(groups):
+        for block in range(width // steps):
+            tiles = [
+                weight_ref[group * width + block * steps + u].astype(jnp.float32)
+                for u in range(steps)
+            ]
+            for a, tile in enumerate(swap_blocks(tiles, TAP_STEP)):
+                mix_ref[
+                    group, a * width : (a + 1) * width, block * LANES : (block + 1) * LANES
+                ] = tile.astype(jnp.bfloat16)
+    span = taps_ref.shape[2]
+    for group in range(groups):
+        rows = slice(group * width, (group + 1) * width)
+        source = column_ref[rows, :].astype(jnp.float32)
+        for a in range(steps):
+            moved = pltpu.roll(source, (span + LANES - a * TAP_STEP) % (span + LANES), 1)
+            shifted_ref[group, a * width : (a + 1) * width, :] = moved[:, :span].astype(
+                jnp.bfloat16
+            )
+    for copy in copies:
+        copy.wait()
+    for group in range(groups):
+        rows = slice(group * width, (group + 1) * width)
+        source = gcol_ref[rows, :].astype(jnp.float32)
+        spread_taps(source, LANES // 2, -1, stage_ref, taps_ref.at[group])
+        product = jnp.dot(mix_ref[group], taps_ref[group], preferred_element_type=jnp.float32)
+        total = product[:width, LANES:]
+        for a in range(1, steps):
+            part = pltpu.roll(product[a * width : (a + 1) * width, :], a * TAP_STEP, 1)
+            total = total + part[:, LANES:]
+        result_ref[rows, :] = total
+    copies = []
+    for step in range(1, count):
+        target = peer(me, step, count)
+        copies.append(
+            remote(
+                result_ref.at[:, lane_block(target)],
+                home_ref.at[row_block(me, channels), :],
+                send_two.at[step],
+                recv_two.at[step],
+                target,
+            )
+        )
+    home_ref[row_block(me, channels), :] = result_ref[:, lane_block(me)]
+    for group in range(groups):
+        grad = lax.dot_general(
+            shifted_ref[group],
+            taps_ref[group],
+            (((1,), (1,)), ((), ())),
+            preferred_element_type=jnp.float32,
+        )
+        for block in range(width // steps):
+            tiles = [
+                grad[a * width : (a + 1) * width, block * LANES : (block + 1) * LANES]
+                for a in range(steps)
+            ]
+            for u, tile in enumerate(swap_blocks(tiles, TAP_STEP)):
+                dweight_ref[group * width + block * steps + u] = tile.astype(dweight_ref.dtype)
+    for copy in copies:
+        copy.wait()
+    back_ref[...] = home_ref[...].T
+
+
+def conv_backward(grad, column, weight, count):
+    tokens, features = grad.shape
+    channels, width, kernel = weight.shape
+    groups = channels // width
+    length = count * LANES
+    span = length + LANES
+    rows = width * TAP_STEP
+    steps = kernel // TAP_STEP
+    sems = [pltpu.SemaphoreType.DMA((count,)) for _ in range(4)]
+    return pl.pallas_call(
+        functools.partial(conv_backward_kernel, count),
+        out_shape=(
+            jax.ShapeDtypeStruct((tokens, features), jnp.float32),
+            jax.ShapeDtypeStruct(weight.shape, jnp.bfloat16),
+        ),
+        in_specs=[VMEM] * 3,
+        out_specs=(VMEM,) * 2,
+        scratch_shapes=[
+            pltpu.VMEM((features, tokens), jnp.bfloat16),
+            pltpu.VMEM((channels, span + LANES), jnp.bfloat16),
+            pltpu.VMEM((channels, length), jnp.float32),
+            pltpu.VMEM((features, tokens), jnp.float32),
+            pltpu.VMEM((span // LANES, rows, LANES), jnp.float32),
+            pltpu.VMEM((groups, rows, span), jnp.bfloat16),
+            pltpu.VMEM((groups, steps * width, rows), jnp.bfloat16),
+            pltpu.VMEM((groups, steps * width, span), jnp.bfloat16),
+        ]
+        + sems,
+        compiler_params=pltpu.CompilerParams(
+            collective_id=1, has_side_effects=True, vmem_limit_bytes=48 * 2**20
+        ),
+        name="conv_backward",
+    )(grad, column, weight)
+
+
+def query_span(index, size):
+    return pl.ds(pl.multiple_of(index * size, size), size)
+
+
+def same_clip(column_ref, seg_row):
+    column = column_ref[...]
+    parts = [
+        column == seg_row[:, start : start + LANES]
+        for start in range(0, seg_row.shape[1], LANES)
+    ]
+    return jnp.concatenate(parts, axis=1)
+
+
+def clip_column(count, segs_ref, column_ref):
+    for block in range(count):
+        row = segs_ref[block].astype(jnp.float32)
+        column_ref[block * LANES : (block + 1) * LANES, :] = jnp.broadcast_to(
+            row, (LANES, LANES)
+        ).T
+
+
+def clip_row(segs_ref, first, size):
+    parts = [segs_ref[first + i].astype(jnp.float32) for i in range(size // LANES)]
+    return jnp.concatenate(parts, axis=1)
+
+
+def attend_forward_kernel(
+    count,
+    head_dim,
+    project_ref,
+    segs_ref,
+    out_ref,
+    main_ref,
+    extra_ref,
+    att_main_ref,
+    att_extra_ref,
+    lse_main_ref,
+    lse_extra_ref,
+    turned_ref,
+    low_main_ref,
+    low_extra_ref,
+    home_ref,
+    column_ref,
+    send_one,
+    recv_one,
+    send_two,
+    recv_two,
+    send_three,
+    recv_three,
+    send_four,
+    recv_four,
+):
+    me = lax.axis_index("blk")
+    features = project_ref.shape[1] // 3
+    length = count * LANES
+    half = count // 2
+    scale = head_dim ** (-0.5)
+    for part in range(3):
+        block = project_ref[:, part * features : (part + 1) * features].astype(jnp.float32)
+        block = block * scale if part == 0 else block
+        turned_ref[part] = block.T.astype(jnp.bfloat16)
+    greet(me, count)
+    copies = []
+    for step in range(1, count):
+        target = peer(me, step, count)
+        copies.append(
+            remote(
+                turned_ref.at[:, row_block(target, head_dim), :],
+                main_ref.at[:, :, lane_block(me)],
+                send_one.at[step],
+                recv_one.at[step],
+                target,
+            )
+        )
+        copies.append(
+            remote(
+                turned_ref.at[:, row_block(count + target // 2, head_dim), :],
+                extra_ref.at[:, :, lane_block(me)],
+                send_two.at[step],
+                recv_two.at[step],
+                target,
+            )
+        )
+    main_ref[:, :, lane_block(me)] = turned_ref[:, row_block(me, head_dim), :]
+    extra_ref[:, :, lane_block(me)] = turned_ref[:, row_block(count + me // 2, head_dim), :]
+    clip_column(count, segs_ref, column_ref)
+    for copy in copies:
+        copy.wait()
+
+    def attend(held_ref, start, seg_row, att_ref, low_ref, lse_ref, place, low_place):
+        size = seg_row.shape[1]
+        queries = held_ref[0, :, start]
+        scores = lax.dot_general(
+            held_ref[1], queries, (((0,), (0,)), ((), ())), preferred_element_type=jnp.float32
+        )
+        scores = jnp.where(same_clip(column_ref, seg_row), scores, -1e30)
+        top = jnp.max(scores, axis=0, keepdims=True)
+        weights = jnp.exp(scores - top)
+        total = jnp.sum(weights, axis=0, keepdims=True)
+        mixed = jnp.dot(
+            held_ref[2], weights.astype(jnp.bfloat16), preferred_element_type=jnp.float32
+        )
+        mixed = mixed / total
+        att_ref[:, place] = mixed
+        low_ref[:, low_place] = mixed.astype(jnp.bfloat16)
+        lse_ref[:, place] = top + jnp.log(total)
+
+    size = 2 * LANES
+    for block in range(length // size):
+        span = slice(block * size, (block + 1) * size)
+        row = clip_row(segs_ref, block * 2, size)
+        attend(main_ref, span, row, att_main_ref, low_main_ref, lse_main_ref, span, span)
+    side = lax.rem(me, 2)
+    for block in range(half * LANES // size):
+        index = side * (half * LANES // size) + block
+        span = query_span(index, size)
+        row = clip_row(segs_ref, index * 2, size)
+        place = slice(block * size, (block + 1) * size)
+        attend(extra_ref, span, row, att_extra_ref, low_extra_ref, lse_extra_ref, place, span)
+
+    own_rows = row_block(me, head_dim)
+    extra_rows = row_block(count + me // 2, head_dim)
+    copies, sides = [], []
+    for step in range(1, count):
+        target = peer(me, step, count)
+        source = peer(me, count - step, count)
+        copies.append(
+            remote(
+                low_main_ref.at[:, lane_block(target)],
+                home_ref.at[own_rows, :],
+                send_three.at[step],
+                recv_three.at[step],
+                target,
+            )
+        )
+        copy = pltpu.make_async_remote_copy(
+            src_ref=low_extra_ref.at[:, lane_block(target)],
+            dst_ref=home_ref.at[extra_rows, :],
+            send_sem=send_four.at[step],
+            recv_sem=recv_four.at[step],
+            device_id={"blk": target},
+            device_id_type=MESH,
+        )
+        sends = target // half == side
+        comes = me // half == lax.rem(source, 2)
+        pl.when(sends)(copy.start)
+        sides.append((sends, comes, copy))
+    home_ref[own_rows, :] = low_main_ref[:, lane_block(me)]
+
+    @pl.when(me // half == side)
+    def _():
+        home_ref[extra_rows, :] = low_extra_ref[:, lane_block(me)]
+
+    for copy in copies:
+        copy.wait()
+    for sends, comes, copy in sides:
+        pl.when(sends)(copy.wait_send)
+        pl.when(comes)(copy.wait_recv)
+    out_ref[...] = home_ref[...].astype(jnp.float32).T.astype(jnp.bfloat16)
+
+
+def attend_forward(project, segs, count, head_dim):
+    tokens, wide = project.shape
+    features = wide // 3
+    length = count * LANES
+    part = length // 2
+    sems = [pltpu.SemaphoreType.DMA((count,)) for _ in range(8)]
+    return pl.pallas_call(
+        functools.partial(attend_forward_kernel, count, head_dim),
+        out_shape=(
+            jax.ShapeDtypeStruct((tokens, features), jnp.bfloat16),
+            jax.ShapeDtypeStruct((3, head_dim, length), jnp.bfloat16),
+            jax.ShapeDtypeStruct((3, head_dim, length), jnp.bfloat16),
+            jax.ShapeDtypeStruct((head_dim, length), jnp.float32),
+            jax.ShapeDtypeStruct((head_dim, part), jnp.float32),
+            jax.ShapeDtypeStruct((1, length), jnp.float32),
+            jax.ShapeDtypeStruct((1, part), jnp.float32),
+        ),
+        in_specs=[VMEM] * 2,
+        out_specs=(VMEM,) * 7,
+        scratch_shapes=[
+            pltpu.VMEM((3, features, tokens), jnp.bfloat16),
+            pltpu.VMEM((head_dim, length), jnp.bfloat16),
+            pltpu.VMEM((head_dim, length), jnp.bfloat16),
+            pltpu.VMEM((features, tokens), jnp.bfloat16),
+            pltpu.VMEM((length, LANES), jnp.float32),
+        ]
+        + sems,
+        compiler_params=pltpu.CompilerParams(
+            collective_id=2, has_side_effects=True, vmem_limit_bytes=48 * 2**20
+        ),
+        name="attend_forward",
+    )(project, segs)
+
+
+def attend_backward_kernel(
+    count,
+    head_dim,
+    grad_ref,
+    segs_ref,
+    main_ref,
+    extra_ref,
+    att_main_ref,
+    att_extra_ref,
+    lse_main_ref,
+    lse_extra_ref,
+    out_ref,
+    turned_ref,
+    gmain_ref,
+    gextra_ref,
+    dmain_ref,
+    dextra_ref,
+    home_ref,
+    part_ref,
+    column_ref,
+    send_one,
+    recv_one,
+    send_two,
+    recv_two,
+    send_three,
+    recv_three,
+    send_four,
+    recv_four,
+    send_five,
+    recv_five,
+):
+    me = lax.axis_index("blk")
+    features = grad_ref.shape[1]
+    length = count * LANES
+    half = count // 2
+    extras = half * head_dim
+    scale = head_dim ** (-0.5)
+    turned_ref[...] = grad_ref[...].astype(jnp.float32).T.astype(jnp.bfloat16)
+    greet(me, count)
+    copies = []
+    for step in range(1, count):
+        target = peer(me, step, count)
+        copies.append(
+            remote(
+                turned_ref.at[row_block(target, head_dim), :],
+                gmain_ref.at[:, lane_block(me)],
+                send_one.at[step],
+                recv_one.at[step],
+                target,
+            )
+        )
+        copies.append(
+            remote(
+                turned_ref.at[row_block(count + target // 2, head_dim), :],
+                gextra_ref.at[:, lane_block(me)],
+                send_two.at[step],
+                recv_two.at[step],
+                target,
+            )
+        )
+    gmain_ref[:, lane_block(me)] = turned_ref[row_block(me, head_dim), :]
+    gextra_ref[:, lane_block(me)] = turned_ref[row_block(count + me // 2, head_dim), :]
+    clip_column(count, segs_ref, column_ref)
+    for copy in copies:
+        copy.wait()
+
+    def attend(held_ref, grad_from, start, seg_row, att, lse):
+        queries = held_ref[0, :, start]
+        grads = grad_from[:, start]
+        scores = lax.dot_general(
+            held_ref[1], queries, (((0,), (0,)), ((), ())), preferred_element_type=jnp.float32
+        )
+        scores = jnp.where(same_clip(column_ref, seg_row), scores, -1e30)
+        weights = jnp.exp(scores - lse)
+        grad_prob = lax.dot_general(
+            held_ref[2], grads, (((0,), (0,)), ((), ())), preferred_element_type=jnp.float32
+        )
+        delta = jnp.sum(grads.astype(jnp.float32) * att, axis=0, keepdims=True)
+        grad_score = (weights * (grad_prob - delta)).astype(jnp.bfloat16)
+        dquery = jnp.dot(held_ref[1], grad_score, preferred_element_type=jnp.float32) * scale
+        dkey = lax.dot_general(
+            queries, grad_score, (((1,), (1,)), ((), ())), preferred_element_type=jnp.float32
+        )
+        dvalue = lax.dot_general(
+            grads,
+            weights.astype(jnp.bfloat16),
+            (((1,), (1,)), ((), ())),
+            preferred_element_type=jnp.float32,
+        )
+        return dquery, dkey, dvalue
+
+    size = 2 * LANES
+    side = lax.rem(me, 2)
+    dkey = dvalue = None
+    for block in range(half * LANES // size):
+        index = side * (half * LANES // size) + block
+        span = query_span(index, size)
+        place = slice(block * size, (block + 1) * size)
+        row = clip_row(segs_ref, index * 2, size)
+        dquery, key_part, value_part = attend(
+            extra_ref, gextra_ref, span, row, att_extra_ref[:, place], lse_extra_ref[:, place]
+        )
+        dextra_ref[0, :, span] = dquery.astype(jnp.bfloat16)
+        dkey = key_part if dkey is None else dkey + key_part
+        dvalue = value_part if dvalue is None else dvalue + value_part
+    dextra_ref[1] = dkey.astype(jnp.bfloat16)
+    dextra_ref[2] = dvalue.astype(jnp.bfloat16)
+
+    own_rows = row_block(me, head_dim)
+    extra_rows = row_block(count + me // 2, head_dim)
+    part_rows = row_block(me // 2, head_dim)
+    copies, sides = [], []
+    for step in range(1, count):
+        target = peer(me, step, count)
+        source = peer(me, count - step, count)
+        copies.append(
+            remote(
+                dextra_ref.at[1:3, :, lane_block(target)],
+                part_ref.at[side, :, part_rows, :],
+                send_three.at[step],
+                recv_three.at[step],
+                target,
+            )
+        )
+        copy = pltpu.make_async_remote_copy(
+            src_ref=dextra_ref.at[0, :, lane_block(target)],
+            dst_ref=home_ref.at[0, extra_rows, :],
+            send_sem=send_four.at[step],
+            recv_sem=recv_four.at[step],
+            device_id={"blk": target},
+            device_id_type=MESH,
+        )
+        sends = target // half == side
+        comes = me // half == lax.rem(source, 2)
+        pl.when(sends)(copy.start)
+        sides.append((sends, comes, copy))
+    part_ref[side, :, part_rows, :] = dextra_ref[1:3, :, lane_block(me)]
+
+    @pl.when(me // half == side)
+    def _():
+        home_ref[0, extra_rows, :] = dextra_ref[0, :, lane_block(me)]
+
+    dkey = dvalue = None
+    for block in range(length // size):
+        span = slice(block * size, (block + 1) * size)
+        row = clip_row(segs_ref, block * 2, size)
+        dquery, key_part, value_part = attend(
+            main_ref, gmain_ref, span, row, att_main_ref[:, span], lse_main_ref[:, span]
+        )
+        dmain_ref[0, :, span] = dquery.astype(jnp.bfloat16)
+        dkey = key_part if dkey is None else dkey + key_part
+        dvalue = value_part if dvalue is None else dvalue + value_part
+    dmain_ref[1] = dkey.astype(jnp.bfloat16)
+    dmain_ref[2] = dvalue.astype(jnp.bfloat16)
+    for step in range(1, count):
+        target = peer(me, step, count)
+        copies.append(
+            remote(
+                dmain_ref.at[:, :, lane_block(target)],
+                home_ref.at[:, own_rows, :],
+                send_five.at[step],
+                recv_five.at[step],
+                target,
+            )
+        )
+    home_ref[:, own_rows, :] = dmain_ref[:, :, lane_block(me)]
+    for copy in copies:
+        copy.wait()
+    for sends, comes, copy in sides:
+        pl.when(sends)(copy.wait_send)
+        pl.when(comes)(copy.wait_recv)
+    first = features - extras
+    for which in range(2):
+        total = part_ref[0, which].astype(jnp.float32) + part_ref[1, which].astype(jnp.float32)
+        home_ref[1 + which, first:, :] = total.astype(jnp.bfloat16)
+    for part in range(3):
+        out_ref[:, part * features : (part + 1) * features] = (
+            home_ref[part].astype(jnp.float32).T.astype(jnp.bfloat16)
+        )
+
+
+def attend_backward(grad, segs, kept, count, head_dim):
+    tokens, features = grad.shape
+    length = count * LANES
+    extras = count // 2 * head_dim
+    sems = [pltpu.SemaphoreType.DMA((count,)) for _ in range(10)]
+    return pl.pallas_call(
+        functools.partial(attend_backward_kernel, count, head_dim),
+        out_shape=jax.ShapeDtypeStruct((tokens, 3 * features), jnp.bfloat16),
+        in_specs=[VMEM] * 8,
+        out_specs=VMEM,
+        scratch_shapes=[
+            pltpu.VMEM((features, tokens), jnp.bfloat16),
+            pltpu.VMEM((head_dim, length), jnp.bfloat16),
+            pltpu.VMEM((head_dim, length), jnp.bfloat16),
+            pltpu.VMEM((3, head_dim, length), jnp.bfloat16),
+            pltpu.VMEM((3, head_dim, length), jnp.bfloat16),
+            pltpu.VMEM((3, features, tokens), jnp.bfloat16),
+            pltpu.VMEM((2, 2, extras, tokens), jnp.bfloat16),
+            pltpu.VMEM((length, LANES), jnp.float32),
+        ]
+        + sems,
+        compiler_params=pltpu.CompilerParams(
+            collective_id=3, has_side_effects=True, vmem_limit_bytes=48 * 2**20
+        ),
+        name="attend_backward",
+    )(grad, segs, *kept)
+
+
+def shards(sizes, *arrays):
+    frames, segment, conv_weight = arrays[:3]
+    row_count, block_len, model_width = frames.shape
+    group_width, kernel = conv_weight.shape[1:]
+    count = sizes["blk"]
+    head_dim = model_width // HEADS
+    channels = model_width // count
+    fits = (
+        row_count == 1
+        and block_len == LANES
+        and kernel == LANES
+        and channels % group_width == 0
+        and group_width % TAP_STEP == 0
+        and count % 4 == 0
+        and 2 * HEADS == 3 * count
+        and head_dim % TAP_STEP == 0
+    )
+    if fits:
+        return swap_shards(count, *arrays)
+    return ring_shards(*arrays)
+
+
+def swap_shards(
+    count,
+    frames,
+    segment,
+    conv_weight,
+    conv_bias,
+    qkv_weight,
+    qv_bias,
+    out_weight,
+    out_bias,
+    norm1_gain,
+    norm1_bias,
+    ffn_in,
+    ffn_in_bias,
+    ffn_out,
+    ffn_out_bias,
+    norm2_gain,
+    norm2_bias,
+    cotangent,
+):
+    _, tokens, width = frames.shape
+    group_width = conv_weight.shape[1]
+    channels = width // count
+    head_dim = width // HEADS
+    me = lax.axis_index("blk")
+    frames = frames[0]
+    own_weight = lax.dynamic_slice_in_dim(conv_weight, me * channels, channels, 0)
+    turned_weight = own_weight.reshape(-1, group_width, *conv_weight.shape[1:])
+    turned_weight = turned_weight.transpose(0, 2, 1, 3)
+    conv_out, column, segs = conv_forward(frames, segment, turned_weight, count)
+    pre_conv = conv_out + conv_bias.astype(jnp.float32)
+    mixed_in = frames.astype(jnp.float32) + gelu_value(pre_conv)
+    mixed_low = mixed_in.astype(jnp.bfloat16)
+    pair_bias = qv_bias.astype(jnp.float32)
+    zero_bias = jnp.zeros((width,), jnp.float32)
+    full_bias = jnp.concatenate([pair_bias[:width], zero_bias, pair_bias[width:]])
+    project = (
+        jnp.dot(mixed_low, qkv_weight, preferred_element_type=jnp.float32) + full_bias
+    ).astype(jnp.bfloat16)
+    attn_low, *kept = attend_forward(project, segs, count, head_dim)
+    branch = jnp.dot(attn_low, out_weight, preferred_element_type=jnp.float32) + out_bias.astype(
+        jnp.float32
+    )
+    gain_one = norm1_gain.astype(jnp.float32)
+    hidden_norm, normed_one, inv_one = norm_forward(
+        mixed_in + branch, gain_one, norm1_bias.astype(jnp.float32)
+    )
+    hidden_low = hidden_norm.astype(jnp.bfloat16)
+    ffn_pre = jnp.dot(hidden_low, ffn_in, preferred_element_type=jnp.float32) + ffn_in_bias.astype(
+        jnp.float32
+    )
+    ffn_act = gelu_value(ffn_pre).astype(jnp.bfloat16)
+    ffn_branch = jnp.dot(
+        ffn_act, ffn_out, preferred_element_type=jnp.float32
+    ) + ffn_out_bias.astype(jnp.float32)
+    gain_two = norm2_gain.astype(jnp.float32)
+    layer_out, normed_two, inv_two = norm_forward(
+        hidden_norm + ffn_branch, gain_two, norm2_bias.astype(jnp.float32)
+    )
+    grad_top = cotangent[0].astype(jnp.float32)
+    grad_second, norm2_gain_grad, norm2_bias_grad = norm_backward(
+        grad_top, normed_two, inv_two, gain_two
+    )
+    grad_branch_two = grad_second.astype(jnp.bfloat16)
+    ffn_out_grad = jnp.einsum(
+        "nf,nd->fd", ffn_act, grad_branch_two, preferred_element_type=jnp.float32
+    )
+    ffn_out_bias_grad = jnp.sum(grad_branch_two.astype(jnp.float32), axis=0)
+    grad_act = jnp.einsum("nd,fd->nf", grad_branch_two, ffn_out, preferred_element_type=jnp.float32)
+    grad_pre = (grad_act * gelu_slope(ffn_pre)).astype(jnp.bfloat16)
+    ffn_in_grad = jnp.einsum("nd,nf->df", hidden_low, grad_pre, preferred_element_type=jnp.float32)
+    ffn_in_bias_grad = jnp.sum(grad_pre.astype(jnp.float32), axis=0)
+    grad_hidden = grad_second + jnp.einsum(
+        "nf,df->nd", grad_pre, ffn_in, preferred_element_type=jnp.float32
+    )
+    grad_first, norm1_gain_grad, norm1_bias_grad = norm_backward(
+        grad_hidden, normed_one, inv_one, gain_one
+    )
+    grad_branch = grad_first.astype(jnp.bfloat16)
+    out_weight_grad = jnp.einsum(
+        "ne,nd->ed", attn_low, grad_branch, preferred_element_type=jnp.float32
+    )
+    out_bias_grad = jnp.sum(grad_branch.astype(jnp.float32), axis=0)
+    grad_att = jnp.einsum(
+        "nd,ed->ne", grad_branch, out_weight, preferred_element_type=jnp.float32
+    ).astype(jnp.bfloat16)
+    grad_project = attend_backward(grad_att, segs, kept, count, head_dim)
+    qkv_weight_grad = jnp.einsum(
+        "nd,ne->de", mixed_low, grad_project, preferred_element_type=jnp.float32
+    )
+    bias_sums = jnp.sum(grad_project.astype(jnp.float32), axis=0)
+    qv_bias_grad = jnp.concatenate([bias_sums[:width], bias_sums[2 * width :]])
+    grad_mixed = grad_first + jnp.einsum(
+        "ne,de->nd", grad_project, qkv_weight, preferred_element_type=jnp.float32
+    )
+    grad_conv = (grad_mixed * gelu_slope(pre_conv)).astype(jnp.bfloat16)
+    conv_bias_grad = jnp.sum(grad_conv.astype(jnp.float32), axis=0)
+    back_conv, conv_weight_grad = conv_backward(grad_conv, column, own_weight, count)
+    is_valid = segment.reshape(tokens, 1) >= 0
+    frames_grad = (grad_mixed + jnp.where(is_valid, back_conv, 0.0)).astype(jnp.bfloat16)
+
+    def summed(grad):
+        part = lax.psum_scatter(
+            grad.astype(jnp.bfloat16), "blk", scatter_dimension=0, tiled=True
+        )
+        return lax.psum(part, "dp").astype(jnp.float32)
+
+    vectors = [
+        conv_bias_grad,
+        qv_bias_grad,
+        out_bias_grad,
+        norm1_gain_grad,
+        norm1_bias_grad,
+        ffn_in_bias_grad,
+        ffn_out_bias_grad,
+        norm2_gain_grad,
+        norm2_bias_grad,
+    ]
+    stacked = jnp.concatenate([vector.reshape(count, -1) for vector in vectors], axis=1)
+    stacked = lax.dynamic_index_in_dim(lax.psum(stacked, ("dp", "blk")), me, 0, keepdims=False)
+    sums, start = [], 0
+    for vector in vectors:
+        size = vector.shape[0] // count
+        sums.append(stacked[start : start + size])
+        start += size
+    return (
+        layer_out.astype(jnp.bfloat16)[None],
+        frames_grad[None],
+        lax.psum(conv_weight_grad, "dp").astype(jnp.float32),
+        sums[0],
+        summed(qkv_weight_grad),
+        sums[1],
+        summed(out_weight_grad),
+        sums[2],
+        sums[3],
+        sums[4],
+        summed(ffn_in_grad),
+        sums[5],
+        summed(ffn_out_grad),
+        sums[6],
+        sums[7],
+        sums[8],
+    )
+
+
 def solution(mesh):
     return jax.shard_map(
-        shards,
+        functools.partial(shards, mesh.shape),
         mesh=mesh,
         in_specs=(
             P("dp", "blk", None),

time: 1530 us -> 546 us (0.36)
  matrix products: 597 us -> 32.1 us
  local copies, waits for them, and re-layouts: 267 us -> 25.6 us
  waiting for transfers between devices: 497 us -> 276 us
  Pallas kernels: 0 us -> 119 us
  other arithmetic: 59.1 us -> 26.2 us
  blocking collectives: 67.1 us -> 42.1 us
  starting transfers between devices: 22 us -> 0.38 us
    conv_general_dilated x3 -> x0, matrix products: 525 us -> none  [the longest x1 205 us: shards(): lax.conv_general_dilated(padded, grad_conv_rows, (1,), 'VALID', dimension...]
    ppermute x44 -> x0, waiting for transfers between devices: 143 us -> none  [the longest x40 143 us: from_behind(): return lax.ppermute(value, axis, pairs)]
    pallas_call x0 -> x4, Pallas kernels: none -> 119 us  [the longest x1 34.1 us: attend_forward(): pl.pallas_call(functools.partial(attend_forward_kernel, count, head_dim),...]
    conv_general_dilated x4 -> x0, local copies, waits for them, and re-layouts: 86 us -> none  [the longest x2 83 us: shards(): lax.conv_general_dilated(padded, grad_conv_rows, (1,), 'VALID', dimension...]
    rev x2 -> x0, local copies, waits for them, and re-layouts: 57.9 us -> none  [shards(): flipped = flipped.reshape(model_width, group_width, kernel)[:, :, ::-1]]
    all_gather x2 -> x0, waiting for transfers between devices: 52.6 us -> none  [the longest x1 45.8 us: shards(): key_piece = lax.all_gather(keys_local, 'blk', axis=1, tiled=True)]
    dot_general x56 -> x12, matrix products: 72 us -> 32.1 us  [the longest x1 5.05 us: swap_shards(): jnp.einsum('nf,nd->fd', ffn_act, grad_branch_two, preferred_element_type=...]
    unnamed x1 -> x0, blocking collectives: 38.8 us -> none
  transfers between devices with their start and end apart: 52 -> 5, of which waited for: 33 -> 4; matrix products, arithmetic and copies ran while one was open for 44% -> 8% of each run, Pallas kernels for 0% -> 11%
where the time goes in v1:
time: 546 us; the launch traced here: 536 us
  waiting for transfers between devices  276 us (51%)
  Pallas kernels  119 us (22%)
  blocking collectives  42.1 us (8%)
  matrix products  32.1 us (6%)
  other arithmetic  26.2 us (5%)
  local copies, waits for them, and re-layouts  25.6 us (5%)
  between operations  14.6 us (3%)
    reduce_scatter x4, waiting for transfers between devices, summed(): lax.psum_scatter(grad.astype(jnp.bfloat16), 'blk', scatter_dimension=0, t...  270 us
    psum x1, blocking collectives, swap_shards(): lax.psum(stacked, ('dp', 'blk'))  42.1 us
    pallas_call x1, Pallas kernels, attend_forward(): pl.pallas_call(functools.partial(attend_forward_kernel, count, head_dim),...  34.1 us
    pallas_call x1, Pallas kernels, attend_backward(): pl.pallas_call(functools.partial(attend_backward_kernel, count, head_dim)...  33.5 us
    pallas_call x1, Pallas kernels, conv_backward(): pl.pallas_call(functools.partial(conv_backward_kernel, count), out_shape=...  27 us
    pallas_call x1, Pallas kernels, conv_forward(): pl.pallas_call(functools.partial(conv_forward_kernel, count), out_shape=(...  24.4 us
  transfers between devices with their start and end apart: 5, of which 4 were waited for; matrix products, arithmetic and copies ran while one was open for 8% of the time, Pallas kernels for 11%

profile of v1, /device:TPU:0, one launch (start us, length us, event | category | flops | bytes accessed | tf_op | source)
XLA Modules:
  0.0 535.9 jit_solution(8101447502688627278)
XLA Ops:
  21.1 24.4 %conv_forward.1 = (f32[128,768]{1,0:T(8,128)S(1)}, bf16[96,1280]{1,0:T(8,128)(2,1)S(1)}, s32[8,1,128]{2,1,0:T(1,128)S(1)}) custom-call(bf16[128,768]{1,0:T(8,128)(2,1)S(1)} %bitcast.72, s32[1,128]{1,0:T(1,128)S(1)} %copy-done.20, bf16[2,48,48,128]{3,2,1,0:T(8,128)(2,1)S(1)} %bitcast.71), custom_call_target="tpu_custom_call" | custom-call | tf_op jit(solution)/shard_map/conv_forward/pallas_call | solution.py:564
  46.3 34.1 %attend_forward.1 = (bf16[128,768]{1,0:T(8,128)(2,1)S(1)}, bf16[3,64,1024]{2,1,0:T(8,128)(2,1)S(1)}, bf16[3,64,1024]{2,1,0:T(8,128)(2,1)S(1)}, f32[64,1024]{1,0:...) custom-call(bf16[128,2304]{1,0:T(8,128)(2,1)S(1)} %fusion.1.project_ref, ...), custom_call_target="tpu_custom_call" | custom-call | tf_op jit(solution)/shard_map/attend_forward/pallas_call | solution.py:896
  82.9 4.3 fusion.39
  88.2 1.5 convert_reduce_fusion.3
  89.7 2.3 convert_reduce_fusion
  92.0 2.3 multiply_reduce_fusion
  95.9 1.5 convolution_convert_fusion.3
  97.5 2.0 convolution_convert_fusion.4.grad_ref
  99.6 33.5 %attend_backward.1 = bf16[128,2304]{1,0:T(8,128)(2,1)S(1)} custom-call(bf16[128,768]{1,0:T(8,128)(2,1)S(1)} %convolution_convert_fusion.4.grad_ref, s32[8,1,128]{2,1,0:T(1,128)S(1)} %get-tuple-element.29.segs_ref, bf16[3,64,1024]{2,1,0:T(8,128)(2,1)S(1)} %copy-done.11, bf16[3,64,1024]{2,1,0:T(8,128)(2,1)S(1)} %copy-done.13, f32[64,1024]{1,0:T(8,128)S(1)} %copy-done.15, ...), custom_call_target="tpu_custom_call" | custom-call | tf_op jit(solution)/shard_map/attend_backward/pallas_call | solution.py:1110
  134.0 3.0 convolution_convert_fusion.2
  137.0 5.0 convolution_convert_fusion
  142.8 4.9 convolution_convert_fusion.1
  148.4 4.0 convert_reduce_fusion.5
  152.4 27.0 %conv_backward.1 = (f32[128,768]{1,0:T(8,128)S(1)}, bf16[96,48,128]{2,1,0:T(8,128)(2,1)S(1)}) custom-call(bf16[128,768]{1,0:T(8,128)(2,1)S(1)} %get-tuple-element.57.grad_ref, bf16[96,1280]{1,0:T(8,128)(2,1)S(1)} %copy-done.17, bf16[96,48,128]{2,1,0:T(8,128)(2,1)S(1)} %copy-done.2), custom_call_target="tpu_custom_call" | custom-call | tf_op jit(solution)/shard_map/conv_backward/pallas_call | solution.py:703
  181.2 73.0 %reduce-scatter.5.cloned.1.call-done = bf16[96,2304]{1,0:T(8,128)(2,1)} async-done(((bf16[768,2304]{1,0:T(8,128)(2,1)}), bf16[96,2304]{1,0:T(8,128)(2,1)}) %reduce-scatter.5.cloned.1.call-update) | async-done | bytes 442384 | tf_op jit(solution)/shard_map/reduce_scatter | solution.py:1257
  254.3 98.5 %reduce-scatter.11.cloned.1.call-done = bf16[384,768]{1,0:T(8,128)(2,1)} async-done(((bf16[3072,768]{1,0:T(8,128)(2,1)}), bf16[384,768]{1,0:T(8,128)(2,1)}) %reduce-scatter.11.cloned.1.call-update) | async-done | bytes 589840 | tf_op jit(solution)/shard_map/reduce_scatter | solution.py:1257
  352.8 98.5 %reduce-scatter.9.cloned.1.call-done = bf16[96,3072]{1,0:T(8,128)(2,1)} async-done(((bf16[768,3072]{1,0:T(8,128)(2,1)}), bf16[96,3072]{1,0:T(8,128)(2,1)}) %reduce-scatter.9.cloned.1.call-update) | async-done | bytes 589840 | tf_op jit(solution)/shard_map/reduce_scatter | solution.py:1257
  466.3 1.4 concatenate.18
  467.7 42.1 %psum.43 = f32[8,1248]{1,0:T(8,128)} all-reduce(f32[8,1248]{1,0:T(8,128)} %concatenate.18), channel_id=1, replica_groups=mesh['dp'=4,'blk'=8] {'dp','blk'}, use_global_device_ids=true, to_apply=%region_18.19 | all-reduce | flops 9984 | bytes 79872 | tf_op jit(solution)/shard_map/psum | solution.py:1274
  513.9 1.9 fusion.25
  515.8 5.8 %all-reduce.3.cloned.1.call-done = (bf16[96,48,128]{2,1,0:T(8,128)(2,1)}, bf16[96,2304]{1,0:T(8,128)(2,1)}, bf16[96,768]{1,0:T(8,128)(2,1)}, bf16[96,3072]{1,0:T(8,128)(2,1)}, bf16[384,768]{1,0:T(8,128)(2,1)}) async-done(((bf16[96,48,128]{2,1,0:T(8,128)(2,1)}, bf16[96,2304]{1,0:T(8,128)(2,1)}, bf16[96,768]{1,0:T(8,128)(2,1)}, bf16[96,3072]{1,0:T(8,128)(2,1)}, bf16[384,768]{1,0:T(8,128)(2,1)}), ...) | async-done | bytes 2949136 | tf_op jit(solution)/shard_map/psum | solution.py:1283
  521.6 1.7 convert_element_type.143
  523.4 2.0 convert_element_type.141
  525.3 1.6 convert_element_type.134
  (166 shorter events, 44.8 us)
Async XLA Ops:
  7.2 38.4 %copy-start = (bf16[768,2304]{1,0:T(8,128)(2,1)S(1)}, bf16[768,2304]{1,0:T(8,128)(2,1)}, u32[]{:S(2)}) copy-start(bf16[768,2304]{1,0:T(8,128)(2,1)} %param.21) | copy-start | bytes 10616836
  7.2 174.0 %reduce-scatter.7.cloned.1.call-start = ((), (), s32[]{:S(2)}) async-start(), calls=%async_computation.5 | async-start | bytes 1327104 | tf_op jit(solution)/shard_map/reduce_scatter | solution.py:1257
  9.4 36.2 %copy-start.33 = (f32[768]{0:T(1024)}, f32[768]{0:T(1024)S(1)}, u32[]{:S(2)}) copy-start(f32[768]{0:T(1024)S(1)} %convert_element_type.112) | copy-start | bytes 9220
  21.1 60.7 %slice-start = ((s8[4718592]{0:T(1024)(128)(4,1)}), s8[4194304]{0:T(1024)(128)(4,1)S(1)}, s32[]{:S(2)}) async-start(s8[4718592]{0:T(1024)(128)(4,1)} %bitcast.73), calls=%async_computation.9 | async-start | bytes 8388608
  45.5 34.9 %copy-start.4 = (f32[128,768]{1,0:T(8,128)}, f32[128,768]{1,0:T(8,128)S(1)}, u32[]{:S(2)}) copy-start(f32[128,768]{1,0:T(8,128)S(1)} %get-tuple-element.28) | copy-start | bytes 1179652
  45.5 34.9 %copy-start.24 = (bf16[768,768]{1,0:T(8,128)(2,1)S(1)}, bf16[768,768]{1,0:T(8,128)(2,1)}, u32[]{:S(2)}) copy-start(bf16[768,768]{1,0:T(8,128)(2,1)} %param.23) | copy-start | bytes 3538948
  45.6 34.9 %copy-start.47 = (f32[768]{0:T(1024)S(1)}, f32[768]{0:T(1024)}, u32[]{:S(2)}) copy-start(f32[768]{0:T(1024)} %convert_element_type.116) | copy-start | bytes 9220
  45.6 36.3 %slice-start.1 = ((s8[4718592]{0:T(1024)(128)(4,1)}), s8[524288]{0:T(1024)(128)(4,1)S(1)}, s32[]{:S(2)}) async-start(s8[4718592]{0:T(1024)(128)(4,1)} %bitcast.73), calls=%async_computation.10 | async-start | bytes 1048576
  46.3 35.6 %copy-start.31 = (f32[768]{0:T(1024)S(1)}, f32[768]{0:T(1024)}, u32[]{:S(2)}) copy-start(f32[768]{0:T(1024)} %convert_element_type.117) | copy-start | bytes 9220
  46.3 35.6 %copy-start.36 = (f32[768]{0:T(1024)S(1)}, f32[768]{0:T(1024)}, u32[]{:S(2)}) copy-start(f32[768]{0:T(1024)} %convert_element_type.118) | copy-start | bytes 9220
  46.3 35.6 %copy-start.38 = (f32[3072]{0:T(1024)S(1)}, f32[3072]{0:T(1024)}, u32[]{:S(2)}) copy-start(f32[3072]{0:T(1024)} %convert_element_type.120) | copy-start | bytes 36868
  81.6 12.7 %copy-start.22 = (f32[128,768]{1,0:T(8,128)}, f32[128,768]{1,0:T(8,128)S(1)}, u32[]{:S(2)}) copy-start(f32[128,768]{1,0:T(8,128)S(1)} %get-tuple-element.71) | copy-start | bytes 1179652
  81.6 12.7 %copy-start.40 = (f32[128]{0:T(128)}, f32[128]{0:T(128)S(1)}, u32[]{:S(2)}) copy-start(f32[128]{0:T(128)S(1)} %broadcast_multiply_fusion.5) | copy-start | bytes 1540
  81.9 12.5 %copy-start.42 = (f32[128]{0:T(128)}, f32[128]{0:T(128)S(1)}, u32[]{:S(2)}) copy-start(f32[128]{0:T(128)S(1)} %add_rsqrt_fusion.1) | copy-start | bytes 1540
  81.9 7.7 %slice-start.2 = ((s8[4718592]{0:T(1024)(128)(4,1)}), s8[4194304]{0:T(1024)(128)(4,1)S(1)}, s32[]{:S(2)}) async-start(s8[4718592]{0:T(1024)(128)(4,1)} %bitcast.75), calls=%async_computation.11 | async-start | bytes 8388608
  82.8 6.8 %copy-start.21 = (f32[128,3072]{1,0:T(8,128)}, f32[128,3072]{1,0:T(8,128)S(1)}, u32[]{:S(2)}) copy-start(f32[128,3072]{1,0:T(8,128)S(1)} %convolution_add_fusion.1) | copy-start | bytes 4718596
  82.9 6.8 %slice-start.3 = ((s8[4718592]{0:T(1024)(128)(4,1)}), s8[524288]{0:T(1024)(128)(4,1)S(1)}, s32[]{:S(2)}) async-start(s8[4718592]{0:T(1024)(128)(4,1)} %bitcast.75), calls=%async_computation.12 | async-start | bytes 1048576
  97.4 156.9 %reduce-scatter.5.cloned.1.call-start = ((), (), s32[]{:S(2)}) async-start(), calls=%async_computation.4 | async-start | bytes 3981312 | tf_op jit(solution)/shard_map/reduce_scatter | solution.py:1257
  97.5 36.5 %copy-start.5 = (f32[128,768]{1,0:T(8,128)S(1)}, f32[128,768]{1,0:T(8,128)}, u32[]{:S(2)}) copy-start(f32[128,768]{1,0:T(8,128)} %copy-done.4) | copy-start | bytes 1179652
  97.5 36.5 %copy-start.7 = (bf16[1,128,768]{2,1,0:T(8,128)(2,1)S(1)}, bf16[1,128,768]{2,1,0:T(8,128)(2,1)}, u32[]{:S(2)}) copy-start(bf16[1,128,768]{2,1,0:T(8,128)(2,1)} %param.17) | copy-start | bytes 589828
  97.5 36.5 %copy-start.34 = (f32[768]{0:T(1024)S(1)}, f32[768]{0:T(1024)}, u32[]{:S(2)}) copy-start(f32[768]{0:T(1024)} %copy-done.33) | copy-start | bytes 9220
  137.0 215.8 %reduce-scatter.11.cloned.1.call-start = ((), (), s32[]{:S(2)}) async-start(), calls=%async_computation.7 | async-start | bytes 5308416 | tf_op jit(solution)/shard_map/reduce_scatter | solution.py:1257
  142.1 309.2 %reduce-scatter.9.cloned.1.call-start = ((), (), s32[]{:S(2)}) async-start(), calls=%async_computation.6 | async-start | bytes 5308416 | tf_op jit(solution)/shard_map/reduce_scatter | solution.py:1257
  147.7 373.9 %all-reduce.3.cloned.1.call-start = ((), (), s32[]{:S(2)}) async-start(), calls=%async_computation.8 | async-start | bytes 5898240 | tf_op jit(solution)/shard_map/psum | solution.py:1283
  (34 other events, 68.5 us)
Sparse Core Ops, SparseCore 0:
  97.5 71.3 reduce-scatter.6
  172.6 81.6 reduce-scatter.4
  257.9 94.8 reduce-scatter.10
  356.3 94.9 reduce-scatter.8
  454.4 67.1 all-reduce.2
